TPU v7x, 512 devices: a whole 4x4x16 slice. The times are simulated.
512 devices in a mesh: row: 16 (over y, x), col: 32 (over z, core).
Axes of the slice: x: 4, y: 4, z: 16, core: 2. Of those that a mesh axis runs over, the one named last changes fastest.
Arguments:
- tile_weights: bfloat16 [16, 32, 32, 128, 128], P('row', 'col'), may hold values from 0 to 4, as said below
- tile_pos: int32 [16, 32, 2, 32], P('row', 'col'), may hold values from 0 to 7, as said below
- tile_total: int32 [16, 32], P('row', 'col'), may hold values from 1 to 32, as said below
- root_ids: int32 [128], replicated, may hold values from 0 to 16383
Outputs:
- hop_level: int32 [16384, 128], P(('row', 'col'))
- path_share: float32 [16384, 128], P(('row', 'col'))
- found_per_level: float32 [4, 128], replicated
Inputs may be any that keep to these rules, and one draw needn't show every extreme that they name: `tile_weights`: nonnegative; an entry is zero wherever the tile has no edge. `tile_pos`: the slots of one device name distinct tile positions; tile rows lie below 8 and tile columns below 4. `tile_total`: some device uses all 32 slots; slots at or past a device's total hold arbitrary positions and zero weights.
All inputs are finite; a program needn't handle non-finite values.
Results may differ from a plain program's by a relative error of at most 0.01.
Values may be sent and summed in bfloat16 or wider, within the bound.
No kernel may reach another device: no remote copies, remote signals or barrier semaphores. Data moves between devices by JAX's collectives and lax.ppermute only.
A program may use at most 64 MiB of HBM per device.

v0:
```python
import jax
import jax.numpy as jnp
from jax import lax
from jax.sharding import Mesh
from jax.sharding import PartitionSpec as P

ROOTS = 128
PV = 32
LEVELS = 4
COL = ("col_0", "col_1")
ROW = ("row_0", "row_1")
ROW_COL = ("row_0", "row_1", "col_0", "col_1")


def sent_to_all(shard, axis):
    devices = lax.axis_size(axis)
    return lax.all_to_all(
        jnp.broadcast_to(shard[None], (devices, *shard.shape)), axis, 0, 0, tiled=True
    )


def joined_along(tiles, dim):
    tiles = jnp.moveaxis(tiles, 0, dim)
    shape = tiles.shape
    return tiles.reshape(*shape[:dim], shape[dim] * shape[dim + 1], *shape[dim + 2 :])


def gather_directly(shard, axis, dim):
    tiles = sent_to_all(shard, axis)
    return joined_along(tiles, dim)


def cut_along(shard, dim, devices):
    shape = shard.shape
    tiles = shard.reshape(*shape[:dim], devices, shape[dim] // devices, *shape[dim + 1 :])
    return jnp.moveaxis(tiles, dim, 0)


def sum_at_owner(shard, axis, dim):
    tiles = cut_along(shard, dim, lax.axis_size(axis))
    arrived = lax.all_to_all(tiles, axis, split_axis=0, concat_axis=0, tiled=True)
    return arrived.astype(jnp.float32).sum(axis=0)


def by_axis(shard, axes):
    for axis in axes:
        shard = lax.psum(shard, axis)
    return shard


def tile_products(source_rows, live_tiles, dest_slots, source_slots, row_tiles):
    source_tiles = source_rows.reshape(-1, 128, source_rows.shape[1])
    blocks = source_tiles[source_slots]
    products = jnp.einsum("src,sck->srk", live_tiles, blocks, preferred_element_type=jnp.float32)
    partial_value = jnp.zeros((row_tiles, 128, source_rows.shape[1]), jnp.float32)
    partial_value = partial_value.at[dest_slots].add(products)
    return partial_value.reshape(row_tiles * 128, source_rows.shape[1])


def local(tile_weights, tile_pos, tile_total, root_ids):
    col_devices = lax.axis_size(COL)
    row_index = lax.axis_index(ROW)
    col_index = lax.axis_index(COL)
    tile_data = tile_weights[0, 0]
    positions = tile_pos[0, 0]
    slot_limit = tile_total[0, 0]
    slot_total = tile_data.shape[0]
    in_use = (jnp.arange(slot_total, dtype=jnp.int32) < slot_limit).astype(jnp.bfloat16)
    live_tiles = tile_data * in_use[:, None, None]
    dest_slots = positions[0]
    source_slots = positions[1]
    row_block = col_devices * PV
    row_tiles = row_block // 128
    state_start = (row_index * col_devices + col_index) * PV
    state_rows = PV
    vertex_ids = state_start + jnp.arange(state_rows, dtype=jnp.int32)
    is_root = vertex_ids[:, None] == root_ids[None, :]
    kept_weight = is_root.astype(jnp.float32)
    path_now = is_root.astype(jnp.bfloat16)
    hop_level = jnp.where(is_root, 0, LEVELS + 1).astype(jnp.int32)
    found_counts = []
    found_totals = []
    for level_num in range(LEVELS):
        own_front = path_now
        source_rows = gather_directly(own_front, ROW, 0)
        partial_value = tile_products(source_rows, live_tiles, dest_slots, source_slots, row_tiles)
        arrived = sum_at_owner(partial_value.astype(jnp.bfloat16), COL, 0)
        newly = (arrived > 0) & (hop_level == LEVELS + 1)
        path_weight = jnp.where(newly, arrived, jnp.float32(0.0))
        hop_level = jnp.where(newly, jnp.int32(level_num + 1), hop_level)
        kept_weight = kept_weight + path_weight
        path_now = path_weight.astype(jnp.bfloat16)
        found_count = jnp.sum(newly.astype(jnp.float32), axis=0)
        found_total = jnp.sum(path_weight, axis=0)
        found_counts.append(found_count)
        found_totals.append(found_total)
    counts = jnp.stack(found_counts)
    totals = jnp.stack(found_totals)
    counts, totals = (by_axis(counts, ROW_COL), by_axis(totals, ROW_COL))
    factor = counts / jnp.maximum(totals, 1.0)
    factor_table = jnp.concatenate(
        [jnp.ones((1, ROOTS), jnp.float32), factor, jnp.zeros((1, ROOTS), jnp.float32)], axis=0
    )
    scale = jnp.zeros_like(kept_weight)
    for level_num in range(LEVELS + 2):
        scale = scale + jnp.where(
            hop_level == level_num, factor_table[level_num][None, :], jnp.float32(0.0)
        )
    return (hop_level, kept_weight * scale, counts)


def solution(mesh):
    torus = Mesh(mesh.devices.reshape(4, 4, 16, 2), ("row_0", "row_1", "col_0", "col_1"))
    return jax.shard_map(
        local,
        mesh=torus,
        in_specs=(P(ROW, COL, None, None, None), P(ROW, COL, None, None), P(ROW, COL), P()),
        out_specs=(P(ROW_COL, None), P(ROW_COL, None), P()),
        check_vma=False,
    )
```

profile of v0, /device:TPU:1, one launch (start us, length us, event | category | flops | bytes accessed | tf_op | source)
XLA Modules:
  0.0 243.6 jit_solution(7852062708470720910)
XLA Ops:
  0.7 0.8 compare_convert_fusion.1
  2.1 7.6 %all-to-all-start = ((bf16[16,32,128]{2,1,0:T(8,128)(2,1)}), bf16[16,32,128]{2,1,0:T(8,128)(2,1)S(1)}, u32[]{:S(2)}, u32[]{:S(2)}) async-start(bf16[16,32,128]{2,1,0:T(8,128)(2,1)} %broadcast_in_dim.109), calls=%async_computation | async-start | bytes 262144 | tf_op jit(solution)/shard_map/all_to_all | solution.py:17
  9.7 0.8 fusion.24
  11.2 5.4 %all-to-all-done = bf16[16,32,128]{2,1,0:T(8,128)(2,1)S(1)} async-done(((bf16[16,32,128]{2,1,0:T(8,128)(2,1)}), bf16[16,32,128]{2,1,0:T(8,128)(2,1)S(1)}, u32[]{:S(2)}, u32[]{:S(2)}) %all-to-all-start) | async-done | bytes 131104 | tf_op jit(solution)/shard_map/all_to_all | solution.py:17
  17.3 1.8 fusion.3
  19.2 4.7 %scatter_fusion = f32[8,128,128]{2,1,0:T(8,128)S(1)} fusion(f32[8,128,128]{2,1,0:T(8,128)S(1)} %broadcast.213.clone.2, s32[32]{0:T(128)S(1)} %get-tuple-element.30, f32[32,128,128]{2,1,0:T(8,128)} %fusion.3), kind=kCustom, calls=%fused_computation.4 | custom fusion | flops 524288 | bytes 6291584 | tf_op jit(solution)/shard_map/scatter-add | solution.py:56
  23.9 39.1 %all_to_all.40 = bf16[32,32,128]{2,1,0:T(8,128)(2,1)S(1)} all-to-all(bf16[32,32,128]{2,1,0:T(8,128)(2,1)S(1)} %bitcast.48), channel_id=1, replica_groups=mesh['row_0'=4,'row_1'=4,'col_0'=16,'col_1'=2] {'col_0','col_1'}, dimensions={0} | all-to-all | bytes 524288 | tf_op jit(solution)/shard_map/all_to_all | solution.py:41
  63.3 9.6 %all_to_all.41 = bf16[16,32,128]{2,1,0:T(8,128)(2,1)S(1)} all-to-all(bf16[16,32,128]{2,1,0:T(8,128)(2,1)S(1)} %broadcast_in_dim.112), channel_id=1, replica_groups=mesh['row_0'=4,'row_1'=4,'col_0'=16,'col_1'=2] {'row_0','row_1'}, dimensions={0} | all-to-all | bytes 262144 | tf_op jit(solution)/shard_map/all_to_all | solution.py:17
  73.7 1.8 fusion.2
  75.5 4.7 %scatter_fusion.1 = f32[8,128,128]{2,1,0:T(8,128)S(1)} fusion(f32[8,128,128]{2,1,0:T(8,128)S(1)} %broadcast.213.clone.1, s32[32]{0:T(128)S(1)} %get-tuple-element.30, f32[32,128,128]{2,1,0:T(8,128)} %fusion.2), kind=kCustom, calls=%fused_computation.5 | custom fusion | flops 524288 | bytes 6291584 | tf_op jit(solution)/shard_map/scatter-add | solution.py:56
  80.3 27.1 %all_to_all.42 = bf16[32,32,128]{2,1,0:T(8,128)(2,1)S(1)} all-to-all(bf16[32,32,128]{2,1,0:T(8,128)(2,1)S(1)} %bitcast.49), channel_id=1, replica_groups=mesh['row_0'=4,'row_1'=4,'col_0'=16,'col_1'=2] {'col_0','col_1'}, dimensions={0} | all-to-all | bytes 524288 | tf_op jit(solution)/shard_map/all_to_all | solution.py:41
  107.5 9.7 %all_to_all.43 = bf16[16,32,128]{2,1,0:T(8,128)(2,1)S(1)} all-to-all(bf16[16,32,128]{2,1,0:T(8,128)(2,1)S(1)} %broadcast_in_dim.114), channel_id=1, replica_groups=mesh['row_0'=4,'row_1'=4,'col_0'=16,'col_1'=2] {'row_0','row_1'}, dimensions={0} | all-to-all | bytes 262144 | tf_op jit(solution)/shard_map/all_to_all | solution.py:17
  117.9 1.8 fusion.1
  119.8 4.7 %scatter_fusion.2 = f32[8,128,128]{2,1,0:T(8,128)S(1)} fusion(f32[8,128,128]{2,1,0:T(8,128)S(1)} %broadcast.213.clone, s32[32]{0:T(128)S(1)} %get-tuple-element.30, f32[32,128,128]{2,1,0:T(8,128)} %fusion.1), kind=kCustom, calls=%fused_computation.6 | custom fusion | flops 524288 | bytes 6291584 | tf_op jit(solution)/shard_map/scatter-add | solution.py:56
  124.5 27.2 %all_to_all.44 = bf16[32,32,128]{2,1,0:T(8,128)(2,1)S(1)} all-to-all(bf16[32,32,128]{2,1,0:T(8,128)(2,1)S(1)} %bitcast.50), channel_id=1, replica_groups=mesh['row_0'=4,'row_1'=4,'col_0'=16,'col_1'=2] {'col_0','col_1'}, dimensions={0} | all-to-all | bytes 524288 | tf_op jit(solution)/shard_map/all_to_all | solution.py:41
  151.9 9.7 %all_to_all.45 = bf16[16,32,128]{2,1,0:T(8,128)(2,1)S(1)} all-to-all(bf16[16,32,128]{2,1,0:T(8,128)(2,1)S(1)} %broadcast_in_dim.116), channel_id=1, replica_groups=mesh['row_0'=4,'row_1'=4,'col_0'=16,'col_1'=2] {'row_0','row_1'}, dimensions={0} | all-to-all | bytes 262144 | tf_op jit(solution)/shard_map/all_to_all | solution.py:17
  161.5 1.7 gather_fusion.3
  163.2 1.7 fusion
  165.0 2.7 %scatter_fusion.3 = f32[8,128,128]{2,1,0:T(8,128)S(1)} fusion(f32[8,128,128]{2,1,0:T(8,128)S(1)} %broadcast.213, s32[32]{0:T(128)S(1)} %get-tuple-element.30, f32[32,128,128]{2,1,0:T(8,128)S(1)} %fusion), kind=kCustom, calls=%fused_computation.7 | custom fusion | flops 524288 | bytes 6291584 | tf_op jit(solution)/shard_map/scatter-add | solution.py:56
  167.7 27.2 %all_to_all.46 = bf16[32,32,128]{2,1,0:T(8,128)(2,1)S(1)} all-to-all(bf16[32,32,128]{2,1,0:T(8,128)(2,1)S(1)} %bitcast.51), channel_id=1, replica_groups=mesh['row_0'=4,'row_1'=4,'col_0'=16,'col_1'=2] {'col_0','col_1'}, dimensions={0} | all-to-all | bytes 524288 | tf_op jit(solution)/shard_map/all_to_all | solution.py:41
  195.0 6.9 %all-reduce.2 = (f32[4,128]{1,0:T(4,128)S(1)}, f32[4,128]{1,0:T(4,128)S(1)}) all-reduce(f32[4,128]{1,0:T(4,128)S(1)} %get-tuple-element.31, f32[4,128]{1,0:T(4,128)S(1)} %get-tuple-element.32), channel_id=1, replica_groups=mesh['row_0'=4,'row_1'=4,'col_0'=16,'col_1'=2] {'row_0'}, use_global_device_ids=true, to_apply=%region_12.13 | all-reduce | flops 1024 | bytes 8192 | tf_op jit(solution)/shard_map/psum | solution.py:47
  202.0 6.6 %all-reduce.1 = (f32[4,128]{1,0:T(4,128)S(1)}, f32[4,128]{1,0:T(4,128)S(1)}) all-reduce(f32[4,128]{1,0:T(4,128)S(1)} %get-tuple-element.15, f32[4,128]{1,0:T(4,128)S(1)} %get-tuple-element.16), channel_id=1, replica_groups=mesh['row_0'=4,'row_1'=4,'col_0'=16,'col_1'=2] {'row_1'}, use_global_device_ids=true, to_apply=%region_13.14 | all-reduce | flops 1024 | bytes 8192 | tf_op jit(solution)/shard_map/psum | solution.py:47
  208.6 20.3 %all-reduce = (f32[4,128]{1,0:T(4,128)S(1)}, f32[4,128]{1,0:T(4,128)S(1)}) all-reduce(f32[4,128]{1,0:T(4,128)S(1)} %get-tuple-element.13, f32[4,128]{1,0:T(4,128)S(1)} %get-tuple-element.14), channel_id=1, replica_groups=mesh['row_0'=4,'row_1'=4,'col_0'=16,'col_1'=2] {'col_0'}, use_global_device_ids=true, to_apply=%region_14.15 | all-reduce | flops 1024 | bytes 8192 | tf_op jit(solution)/shard_map/psum | solution.py:47
  228.9 14.0 %all-reduce.3 = (f32[4,128]{1,0:T(4,128)S(1)}, f32[4,128]{1,0:T(4,128)S(1)}) all-reduce(f32[4,128]{1,0:T(4,128)S(1)} %get-tuple-element.11, f32[4,128]{1,0:T(4,128)S(1)} %get-tuple-element.12), channel_id=1, replica_groups=mesh['row_0'=4,'row_1'=4,'col_0'=16,'col_1'=2] {'col_1'}, use_global_device_ids=true, to_apply=%region_15.16 | all-reduce | flops 1024 | bytes 8192 | tf_op jit(solution)/shard_map/psum | solution.py:47
  (39 shorter events, 4.6 us)
Async XLA Ops:
  0.6 16.7 %copy-start = (bf16[1,1,32,128,128]{4,3,2,1,0:T(8,128)(2,1)S(1)}, bf16[1,1,32,128,128]{4,3,2,1,0:T(8,128)(2,1)}, u32[]{:S(2)}) copy-start(bf16[1,1,32,128,128]{4,3,2,1,0:T(8,128)(2,1)} %param.4) | copy-start | bytes 3145732
  2.1 14.4 %all-to-all-start = ((bf16[16,32,128]{2,1,0:T(8,128)(2,1)}), bf16[16,32,128]{2,1,0:T(8,128)(2,1)S(1)}, u32[]{:S(2)}, u32[]{:S(2)}) async-start(bf16[16,32,128]{2,1,0:T(8,128)(2,1)} %broadcast_in_dim.109), calls=%async_computation | async-start | bytes 262144 | tf_op jit(solution)/shard_map/all_to_all | solution.py:17
  19.2 43.9 %copy-start.1 = (s32[128]{0:T(128)S(1)}, s32[128]{0:T(128)}, u32[]{:S(2)}) copy-start(s32[128]{0:T(128)} %param.7) | copy-start | bytes 1540
  242.8 0.7 copy-start.2
where the time goes:
time: 244 us
  blocking collectives  197 us (81%)
  other arithmetic  19.7 us (8%)
  starting transfers between devices  7.58 us (3%)
  matrix products  7.22 us (3%)
  waiting for transfers between devices  5.4 us (2%)
  local copies, waits for them, and re-layouts  4.79 us (2%)
    all_to_all x4, blocking collectives, sum_at_owner(): lax.all_to_all(tiles, axis, split_axis=0, concat_axis=0, tiled=True)  121 us
    psum x4, blocking collectives, by_axis(): shard = lax.psum(shard, axis)  47.8 us
    all_to_all x3, blocking collectives, sent_to_all(): lax.all_to_all(jnp.broadcast_to(shard[None], (devices, *shard.shape)), ax...  29 us
    scatter-add x4, other arithmetic, tile_products(): partial_value = partial_value.at[dest_slots].add(products)  16.7 us
    all_to_all x1, starting transfers between devices, sent_to_all(): lax.all_to_all(jnp.broadcast_to(shard[None], (devices, *shard.shape)), ax...  7.58 us
    dot_general x4, matrix products, tile_products(): jnp.einsum('src,sck->srk', live_tiles, blocks, preferred_element_type=jnp...  7.22 us
    all_to_all x1, waiting for transfers between devices, sent_to_all(): lax.all_to_all(jnp.broadcast_to(shard[None], (devices, *shard.shape)), ax...  5.4 us
  transfers between devices with their start and end apart: 1, of which 1 were waited for; matrix products, arithmetic and copies ran while one was open for 0% of the time, Pallas kernels for 0%

commit v1 on v0

--- a/solution.py
+++ b/solution.py
@@ -44,7 +44,7 @@
 
 def by_axis(shard, axes):
     for axis in axes:
-        shard = lax.psum(shard, axis)
+        shard = jnp.sum(lax.all_gather(shard, axis), axis=0)
     return shard
 
 

time: 244 us -> 297 us (1.22)
  blocking collectives: 197 us -> 250 us
    all_gather x0 -> x8, blocking collectives: none -> 100 us  [by_axis(): shard = jnp.sum(lax.all_gather(shard, axis), axis=0)]
    psum x4 -> x0, blocking collectives: 47.8 us -> none  [by_axis(): shard = lax.psum(shard, axis)]
where the time goes in v1:
time: 297 us; the launch traced here: 296 us
  blocking collectives  250 us (84%)
  other arithmetic  19.8 us (7%)
  starting transfers between devices  7.58 us (3%)
  matrix products  7.22 us (2%)
  waiting for transfers between devices  5.4 us (2%)
  local copies, waits for them, and re-layouts  4.79 us (2%)
    all_to_all x4, blocking collectives, sum_at_owner(): lax.all_to_all(tiles, axis, split_axis=0, concat_axis=0, tiled=True)  121 us
    all_gather x8, blocking collectives, by_axis(): shard = jnp.sum(lax.all_gather(shard, axis), axis=0)  100 us
    all_to_all x3, blocking collectives, sent_to_all(): lax.all_to_all(jnp.broadcast_to(shard[None], (devices, *shard.shape)), ax...  29 us
    scatter-add x4, other arithmetic, tile_products(): partial_value = partial_value.at[dest_slots].add(products)  16.7 us
    all_to_all x1, starting transfers between devices, sent_to_all(): lax.all_to_all(jnp.broadcast_to(shard[None], (devices, *shard.shape)), ax...  7.58 us
    dot_general x4, matrix products, tile_products(): jnp.einsum('src,sck->srk', live_tiles, blocks, preferred_element_type=jnp...  7.22 us
  transfers between devices with their start and end apart: 1, of which 1 were waited for; matrix products, arithmetic and copies ran while one was open for 0% of the time, Pallas kernels for 0%

profile of v1, /device:TPU:1, one launch (start us, length us, event | category | flops | bytes accessed | tf_op | source)
XLA Modules:
  0.0 296.1 jit_solution(6308103931941374257)
XLA Ops:
  2.1 7.6 %all-to-all-start = ((bf16[16,32,128]{2,1,0:T(8,128)(2,1)}), bf16[16,32,128]{2,1,0:T(8,128)(2,1)S(1)}, u32[]{:S(2)}, u32[]{:S(2)}) async-start(bf16[16,32,128]{2,1,0:T(8,128)(2,1)} %broadcast_in_dim.109), calls=%async_computation | async-start | bytes 262144 | tf_op jit(solution)/shard_map/all_to_all | solution.py:17
  11.2 5.4 %all-to-all-done = bf16[16,32,128]{2,1,0:T(8,128)(2,1)S(1)} async-done(((bf16[16,32,128]{2,1,0:T(8,128)(2,1)}), bf16[16,32,128]{2,1,0:T(8,128)(2,1)S(1)}, u32[]{:S(2)}, u32[]{:S(2)}) %all-to-all-start) | async-done | bytes 131104 | tf_op jit(solution)/shard_map/all_to_all | solution.py:17
  17.3 1.8 fusion.3
  19.2 4.7 %scatter_fusion = f32[8,128,128]{2,1,0:T(8,128)S(1)} fusion(f32[8,128,128]{2,1,0:T(8,128)S(1)} %broadcast.213.clone.2, s32[32]{0:T(128)S(1)} %get-tuple-element.22, f32[32,128,128]{2,1,0:T(8,128)} %fusion.3), kind=kCustom, calls=%fused_computation.4 | custom fusion | flops 524288 | bytes 6291584 | tf_op jit(solution)/shard_map/scatter-add | solution.py:56
  23.9 39.1 %all_to_all.40 = bf16[32,32,128]{2,1,0:T(8,128)(2,1)S(1)} all-to-all(bf16[32,32,128]{2,1,0:T(8,128)(2,1)S(1)} %bitcast.58), channel_id=1, replica_groups=mesh['row_0'=4,'row_1'=4,'col_0'=16,'col_1'=2] {'col_0','col_1'}, dimensions={0} | all-to-all | bytes 524288 | tf_op jit(solution)/shard_map/all_to_all | solution.py:41
  63.3 9.6 %all_to_all.41 = bf16[16,32,128]{2,1,0:T(8,128)(2,1)S(1)} all-to-all(bf16[16,32,128]{2,1,0:T(8,128)(2,1)S(1)} %broadcast_in_dim.112), channel_id=1, replica_groups=mesh['row_0'=4,'row_1'=4,'col_0'=16,'col_1'=2] {'row_0','row_1'}, dimensions={0} | all-to-all | bytes 262144 | tf_op jit(solution)/shard_map/all_to_all | solution.py:17
  73.7 1.8 fusion.2
  75.5 4.7 %scatter_fusion.1 = f32[8,128,128]{2,1,0:T(8,128)S(1)} fusion(f32[8,128,128]{2,1,0:T(8,128)S(1)} %broadcast.213.clone.1, s32[32]{0:T(128)S(1)} %get-tuple-element.22, f32[32,128,128]{2,1,0:T(8,128)} %fusion.2), kind=kCustom, calls=%fused_computation.5 | custom fusion | flops 524288 | bytes 6291584 | tf_op jit(solution)/shard_map/scatter-add | solution.py:56
  80.3 27.1 %all_to_all.42 = bf16[32,32,128]{2,1,0:T(8,128)(2,1)S(1)} all-to-all(bf16[32,32,128]{2,1,0:T(8,128)(2,1)S(1)} %bitcast.59), channel_id=1, replica_groups=mesh['row_0'=4,'row_1'=4,'col_0'=16,'col_1'=2] {'col_0','col_1'}, dimensions={0} | all-to-all | bytes 524288 | tf_op jit(solution)/shard_map/all_to_all | solution.py:41
  107.5 9.7 %all_to_all.43 = bf16[16,32,128]{2,1,0:T(8,128)(2,1)S(1)} all-to-all(bf16[16,32,128]{2,1,0:T(8,128)(2,1)S(1)} %broadcast_in_dim.114), channel_id=1, replica_groups=mesh['row_0'=4,'row_1'=4,'col_0'=16,'col_1'=2] {'row_0','row_1'}, dimensions={0} | all-to-all | bytes 262144 | tf_op jit(solution)/shard_map/all_to_all | solution.py:17
  117.9 1.8 fusion.1
  119.8 4.7 %scatter_fusion.2 = f32[8,128,128]{2,1,0:T(8,128)S(1)} fusion(f32[8,128,128]{2,1,0:T(8,128)S(1)} %broadcast.213.clone, s32[32]{0:T(128)S(1)} %get-tuple-element.22, f32[32,128,128]{2,1,0:T(8,128)} %fusion.1), kind=kCustom, calls=%fused_computation.6 | custom fusion | flops 524288 | bytes 6291584 | tf_op jit(solution)/shard_map/scatter-add | solution.py:56
  124.5 27.2 %all_to_all.44 = bf16[32,32,128]{2,1,0:T(8,128)(2,1)S(1)} all-to-all(bf16[32,32,128]{2,1,0:T(8,128)(2,1)S(1)} %bitcast.60), channel_id=1, replica_groups=mesh['row_0'=4,'row_1'=4,'col_0'=16,'col_1'=2] {'col_0','col_1'}, dimensions={0} | all-to-all | bytes 524288 | tf_op jit(solution)/shard_map/all_to_all | solution.py:41
  151.9 9.7 %all_to_all.45 = bf16[16,32,128]{2,1,0:T(8,128)(2,1)S(1)} all-to-all(bf16[16,32,128]{2,1,0:T(8,128)(2,1)S(1)} %broadcast_in_dim.116), channel_id=1, replica_groups=mesh['row_0'=4,'row_1'=4,'col_0'=16,'col_1'=2] {'row_0','row_1'}, dimensions={0} | all-to-all | bytes 262144 | tf_op jit(solution)/shard_map/all_to_all | solution.py:17
  165.0 2.7 scatter_fusion.3
  167.7 27.2 %all_to_all.46 = bf16[32,32,128]{2,1,0:T(8,128)(2,1)S(1)} all-to-all(bf16[32,32,128]{2,1,0:T(8,128)(2,1)S(1)} %bitcast.61), channel_id=1, replica_groups=mesh['row_0'=4,'row_1'=4,'col_0'=16,'col_1'=2] {'col_0','col_1'}, dimensions={0} | all-to-all | bytes 524288 | tf_op jit(solution)/shard_map/all_to_all | solution.py:41
  195.0 8.1 %all-gather.12 = f32[4,4,128]{2,1,0:T(4,128)S(1)} all-gather(f32[1,4,128]{2,1,0:T(4,128)S(1)} %maximum_bitcast_fusion.1), channel_id=6, replica_groups=mesh['row_0'=4,'row_1'=4,'col_0'=16,'col_1'=2] {'row_0'}, dimensions={0}, use_global_device_ids=true | all-gather | bytes 10240 | tf_op jit(solution)/shard_map/all_gather | solution.py:47
  203.1 8.1 %all-gather.13 = f32[4,4,128]{2,1,0:T(4,128)S(1)} all-gather(f32[1,4,128]{2,1,0:T(4,128)S(1)} %bitcast.64), channel_id=7, replica_groups=mesh['row_0'=4,'row_1'=4,'col_0'=16,'col_1'=2] {'row_1'}, dimensions={0}, use_global_device_ids=true | all-gather | bytes 10240 | tf_op jit(solution)/shard_map/all_gather | solution.py:47
  211.2 19.1 %all-gather.14 = f32[16,4,128]{2,1,0:T(4,128)S(1)} all-gather(f32[1,4,128]{2,1,0:T(4,128)S(1)} %bitcast.65), channel_id=8, replica_groups=mesh['row_0'=4,'row_1'=4,'col_0'=16,'col_1'=2] {'col_0'}, dimensions={0}, use_global_device_ids=true | all-gather | bytes 34816 | tf_op jit(solution)/shard_map/all_gather | solution.py:47
  230.4 14.2 %all-gather.15 = f32[2,4,128]{2,1,0:T(4,128)S(1)} all-gather(f32[1,4,128]{2,1,0:T(4,128)S(1)} %bitcast.62), channel_id=9, replica_groups=mesh['row_0'=4,'row_1'=4,'col_0'=16,'col_1'=2] {'col_1'}, dimensions={0}, use_global_device_ids=true | all-gather | bytes 6144 | tf_op jit(solution)/shard_map/all_gather | solution.py:47
  244.5 8.1 %all-gather.8 = f32[4,4,128]{2,1,0:T(4,128)S(1)} all-gather(f32[1,4,128]{2,1,0:T(4,128)S(1)} %maximum_bitcast_fusion), channel_id=2, replica_groups=mesh['row_0'=4,'row_1'=4,'col_0'=16,'col_1'=2] {'row_0'}, dimensions={0}, use_global_device_ids=true | all-gather | bytes 10240 | tf_op jit(solution)/shard_map/all_gather | solution.py:47
  252.6 8.1 %all-gather.9 = f32[4,4,128]{2,1,0:T(4,128)S(1)} all-gather(f32[1,4,128]{2,1,0:T(4,128)S(1)} %bitcast.66), channel_id=3, replica_groups=mesh['row_0'=4,'row_1'=4,'col_0'=16,'col_1'=2] {'row_1'}, dimensions={0}, use_global_device_ids=true | all-gather | bytes 10240 | tf_op jit(solution)/shard_map/all_gather | solution.py:47
  260.7 21.1 %all-gather.10 = f32[16,4,128]{2,1,0:T(4,128)S(1)} all-gather(f32[1,4,128]{2,1,0:T(4,128)S(1)} %bitcast.67), channel_id=4, replica_groups=mesh['row_0'=4,'row_1'=4,'col_0'=16,'col_1'=2] {'col_0'}, dimensions={0}, use_global_device_ids=true | all-gather | bytes 34816 | tf_op jit(solution)/shard_map/all_gather | solution.py:47
  281.8 13.5 %all-gather.11 = f32[2,4,128]{2,1,0:T(4,128)S(1)} all-gather(f32[1,4,128]{2,1,0:T(4,128)S(1)} %bitcast.63), channel_id=5, replica_groups=mesh['row_0'=4,'row_1'=4,'col_0'=16,'col_1'=2] {'col_1'}, dimensions={0}, use_global_device_ids=true | all-gather | bytes 6144 | tf_op jit(solution)/shard_map/all_gather | solution.py:47
  (52 shorter events, 9.7 us)
Async XLA Ops:
  0.6 16.7 %copy-start = (bf16[1,1,32,128,128]{4,3,2,1,0:T(8,128)(2,1)S(1)}, bf16[1,1,32,128,128]{4,3,2,1,0:T(8,128)(2,1)}, u32[]{:S(2)}) copy-start(bf16[1,1,32,128,128]{4,3,2,1,0:T(8,128)(2,1)} %param.4) | copy-start | bytes 3145732
  2.1 14.4 %all-to-all-start = ((bf16[16,32,128]{2,1,0:T(8,128)(2,1)}), bf16[16,32,128]{2,1,0:T(8,128)(2,1)S(1)}, u32[]{:S(2)}, u32[]{:S(2)}) async-start(bf16[16,32,128]{2,1,0:T(8,128)(2,1)} %broadcast_in_dim.109), calls=%async_computation | async-start | bytes 262144 | tf_op jit(solution)/shard_map/all_to_all | solution.py:17
  19.2 43.9 %copy-start.1 = (s32[128]{0:T(128)S(1)}, s32[128]{0:T(128)}, u32[]{:S(2)}) copy-start(s32[128]{0:T(128)} %param.7) | copy-start | bytes 1540
  295.4 0.7 copy-start.2
